TPU v7x, 32 devices: a whole 2x2x4 slice. The times are simulated.
32 devices in a mesh: grp: 4 (over z), feat: 8 (over y, x, core).
Axes of the slice: x: 2, y: 2, z: 4, core: 2. Of those that a mesh axis runs over, the one named last changes fastest.
Arguments:
- features: bfloat16 [8192, 512], P(('grp', 'feat')), may hold values from -6 to 6
- adj_tiles: bfloat16 [64, 16, 128, 128], P(('grp', 'feat')), may hold values from 0.0099487305 to 1
- src_block: int32 [64, 16], P(('grp', 'feat')), may hold values from 0 to 15, as said below
- counts: int32 [64], P(('grp', 'feat')), may hold values from 1 to 16, as said below
- w_self: bfloat16 [512, 512], replicated, may hold values from -0.25 to 0.25
- w_neigh: bfloat16 [512, 512], replicated, may hold values from -0.25 to 0.25
- multiplier: float32 [512], replicated, may hold values from 0.5 to 2
- bit_shift: int32 [512], replicated, may hold values from 0 to 2
- cotangent: bfloat16 [8192, 512], P(('grp', 'feat')), may hold values from -6 to 6
Outputs:
- output: bfloat16 [8192, 512], P(('grp', 'feat'))
- grad_features: bfloat16 [8192, 512], P(('grp', 'feat'))
- grad_self: float32 [512, 512], replicated
- grad_neigh: float32 [512, 512], replicated
Inputs may be any that keep to these rules, and one draw needn't show every extreme that they name: src_block[i, k] is a block of block i's own group, held by a device at most 2 positions from block i's device in the group's cyclic order of devices (block i is held by device (i % 16) // 2 of its group, which holds 2 consecutive blocks); the distance 2 is reached in both directions in every draw. Slots k >= counts[i] take no part.
All inputs are finite; a program needn't handle non-finite values.
Results may differ from a plain program's by a relative error of at most 0.0059.
Values may be sent and summed in bfloat16 or wider, within the bound.
A program may use at most 64 MiB of HBM per device.

v0:
```python
import math

import jax
import jax.numpy as jnp
from jax import lax
from jax.sharding import PartitionSpec as P

SPAN = 2


def passed_along(x, axis, by):
    peers = lax.axis_size(axis)
    return lax.ppermute(x, axis, [(i, (i + by) % peers) for i in range(peers)])


def fetch_near(shard_piece, steps_by):
    return passed_along(shard_piece, "feat", steps_by)


def return_near(shard_piece, steps_by):
    return passed_along(shard_piece, "feat", steps_by)


def local(
    features, adj_tiles, src_block, counts, w_self, w_neigh, multiplier, bit_shift, cotangent
):
    num_blocks = adj_tiles.shape[0]
    num_slots = adj_tiles.shape[1]
    block_len = adj_tiles.shape[2]
    feature_width = features.shape[1]
    row_count = features.shape[0]
    feat_count = lax.axis_size("feat")
    my_index = lax.axis_index("feat")
    live_mask = jnp.arange(num_slots, dtype=jnp.int32)[None, :] < counts[:, None]
    masked = jnp.where(live_mask[:, :, None, None], adj_tiles, jnp.zeros_like(adj_tiles))
    degree = jnp.sum(masked, axis=(1, 3), dtype=jnp.float32)
    inv_root = lax.rsqrt(degree)
    node_blocks = features.reshape(num_blocks, block_len, feature_width)
    pieces = {0: node_blocks}
    for offset in range(-SPAN, SPAN + 1):
        if offset != 0:
            pieces[offset] = fetch_near(node_blocks, -offset)
    source_pool = jnp.concatenate([pieces[offset] for offset in range(-SPAN, SPAN + 1)], axis=0)
    relative = (src_block // num_blocks - my_index + SPAN) % feat_count
    slot_index = relative * num_blocks + src_block % num_blocks
    flat_index = slot_index.reshape(-1)
    sources = jnp.take(source_pool, flat_index, axis=0).reshape(
        num_blocks, num_slots, block_len, feature_width
    )
    summed = jnp.einsum("bkij,bkjf->bif", masked, sources, preferred_element_type=jnp.float32)
    aggregated = (
        (summed * inv_root[:, :, None]).astype(jnp.bfloat16).reshape(row_count, feature_width)
    )
    preact = jnp.dot(features, w_self, preferred_element_type=jnp.float32)
    preact = preact + jnp.dot(aggregated, w_neigh, preferred_element_type=jnp.float32)
    scale = multiplier * jnp.exp2(-bit_shift.astype(jnp.float32))
    scaled = preact * scale
    sigmoid_val = jax.nn.sigmoid(scaled)
    output = (scaled * sigmoid_val).astype(jnp.bfloat16)
    grad_pre = (
        cotangent.astype(jnp.float32) * sigmoid_val * (1.0 + scaled * (1.0 - sigmoid_val)) * scale
    ).astype(jnp.bfloat16)
    part_self = jnp.dot(features.T, grad_pre, preferred_element_type=jnp.float32)
    part_neigh = jnp.dot(aggregated.T, grad_pre, preferred_element_type=jnp.float32)
    total_self, total_neigh = lax.psum((part_self, part_neigh), ("grp", "feat"))
    grad_scale = 1.0 / math.sqrt(row_count * lax.axis_size("grp") * feat_count)
    own_part = jnp.dot(grad_pre, w_self.T, preferred_element_type=jnp.float32)
    back = jnp.dot(grad_pre, w_neigh.T, preferred_element_type=jnp.float32).reshape(
        num_blocks, block_len, feature_width
    )
    back = (back * inv_root[:, :, None]).astype(jnp.bfloat16)
    contrib = jnp.einsum("bkij,bif->bkjf", masked, back, preferred_element_type=jnp.float32)
    contrib_flat = contrib.reshape(num_blocks * num_slots, block_len * feature_width)
    window_count = (2 * SPAN + 1) * num_blocks
    grouped = jax.ops.segment_sum(contrib_flat, flat_index, num_segments=window_count)
    window = lax.optimization_barrier(grouped.astype(jnp.bfloat16))
    window = window.reshape(window_count, block_len, feature_width)

    def window_piece(offset):
        first_block = (offset + SPAN) * num_blocks
        return window[first_block : first_block + num_blocks]

    spread_blocks = window_piece(0).astype(jnp.float32)
    for offset in range(-SPAN, SPAN + 1):
        if offset != 0:
            arrived = return_near(window_piece(offset), offset)
            spread_blocks = spread_blocks + arrived.astype(jnp.float32)
    spread = spread_blocks.reshape(row_count, feature_width)
    grad_features = (own_part + spread).astype(jnp.bfloat16)
    return (output, grad_features, total_self * grad_scale, total_neigh * grad_scale)


def solution(mesh):
    return jax.shard_map(
        local,
        mesh=mesh,
        in_specs=(
            P(("grp", "feat"), None),
            P(("grp", "feat"), None, None, None),
            P(("grp", "feat"), None),
            P(("grp", "feat")),
            P(),
            P(),
            P(),
            P(),
            P(("grp", "feat"), None),
        ),
        out_specs=(P(("grp", "feat"), None), P(("grp", "feat"), None), P(), P()),
        check_vma=False,
    )
```

profile of v0, /device:TPU:1, one launch (start us, length us, event | category | flops | bytes accessed | tf_op | source)
XLA Modules:
  0.0 274.0 jit_solution(16146339780754141615)
XLA Ops:
  7.2 2.1 collective-permute-start
  9.3 2.1 collective-permute-start.1
  11.4 1.2 collective-permute-start.3
  12.6 0.7 compare_and_fusion
  13.4 0.7 iota_compare_fusion
  14.1 2.2 fusion.33
  17.0 1.6 convert_reduce_fusion
  18.8 1.5 collective-permute-done.1
  20.3 3.8 %collective-permute-done.2 = bf16[2,128,512]{2,1,0:T(8,128)(2,1)S(1)} collective-permute-done((bf16[2,128,512]{2,1,0:T(8,128)(2,1)}, bf16[2,128,512]{2,1,0:T(8,128)(2,1)S(1)}, u32[]{:S(2)}, u32[]{:S(2)}) %collective-permute-start.2) | collective-permute-done | bytes 262176 | tf_op jit(solution)/shard_map/ppermute | solution.py:13
  24.1 3.6 %collective-permute-done.3 = bf16[2,128,512]{2,1,0:T(8,128)(2,1)S(1)} collective-permute-done((bf16[2,128,512]{2,1,0:T(8,128)(2,1)}, bf16[2,128,512]{2,1,0:T(8,128)(2,1)S(1)}, u32[]{:S(2)}, u32[]{:S(2)}) %collective-permute-start.3) | collective-permute-done | bytes 262176 | tf_op jit(solution)/shard_map/ppermute | solution.py:13
  27.7 2.8 %gather_fusion = bf16[32,128,512]{2,1,0:T(8,128)(2,1)} fusion(bf16[10,128,512]{2,1,0:T(8,128)(2,1)S(1)} %constant_dynamic-update-slice_fusion, s32[1024]{0:T(1024)S(1)} %pad_clamp_fusion), kind=kCustom, calls=%fused_computation | custom fusion | bytes 8388736 | tf_op jit(solution)/shard_map/jit(_take)/gather | solution.py:47
  30.5 3.1 %fusion.11 = bf16[2,128,512]{2,1,0:T(8,128)(2,1)S(1)} fusion(bf16[2,16,128,512]{3,2,1,0:T(8,128)(2,1)} %bitcast.66, pred[2,16]{1,0:T(4,128)(4,1)S(1)} %get-tuple-element.10, bf16[2,16,128,128]{3,2,1,0:T(8,128)(2,1)S(1)} %copy-done.1, pred[2,16]{1,0:T(4,128)(4,1)S(1)} %iota_compare_fusion, f32[2,128]{1,0:T(2,128)S(1)} %rsqrt.7), kind=kOutput, calls=%fused_computation.12 | convolution fusion | flops 539754496 | bytes 5506112 | tf_op jit(solution)/shard_map/bkij,bkjf->bif/dot_general | solution.py:50
  33.6 1.2 multiply_convert_fusion.1
  34.9 1.3 fusion.35
  36.2 1.3 convolution_bitcast_fusion
  37.8 1.4 fusion.14
  39.2 8.1 %copy.21 = f32[4,8,128,512]{3,1,2,0:T(8,128)} copy(f32[4,8,128,512]{3,2,1,0:T(8,128)S(1)} %bitcast.65) | data formatting | bytes 16777216
  47.3 2.2 broadcast_in_dim.35
  49.6 76.0 %scatter_fusion = f32[10,65536]{1,0:T(8,128)} fusion(f32[10,65536]{1,0:T(8,128)} %broadcast_in_dim.35, s32[32]{0:T(128)S(1)} %reshape.113, f32[32,65536]{1,0:T(8,128)} %bitcast.64), kind=kCustom, calls=%fused_computation.1 | custom fusion | flops 2097152 | bytes 25165952 | tf_op jit(solution)/shard_map/scatter-add | solution.py:75
  125.6 2.4 convert_element_type.52
  128.0 0.8 fusion.32
  128.9 1.3 collective-permute-start.4
  130.2 1.9 collective-permute-start.5
  132.2 1.9 collective-permute-start.7
  134.2 1.1 collective-permute-done.4
  135.3 12.7 %collective-permute-done.5 = bf16[2,128,512]{2,1,0:T(8,128)(2,1)S(1)} collective-permute-done((bf16[2,128,512]{2,1,0:T(8,128)(2,1)S(1)}, bf16[2,128,512]{2,1,0:T(8,128)(2,1)S(1)}, u32[]{:S(2)}, u32[]{:S(2)}) %collective-permute-start.5) | collective-permute-done | bytes 262176 | tf_op jit(solution)/shard_map/ppermute | solution.py:13
  148.0 3.0 %collective-permute-done.7 = bf16[2,128,512]{2,1,0:T(8,128)(2,1)S(1)} collective-permute-done((bf16[2,128,512]{2,1,0:T(8,128)(2,1)S(1)}, bf16[2,128,512]{2,1,0:T(8,128)(2,1)S(1)}, u32[]{:S(2)}, u32[]{:S(2)}) %collective-permute-start.7) | collective-permute-done | bytes 262176 | tf_op jit(solution)/shard_map/ppermute | solution.py:13
  151.2 1.0 fusion.18
  152.2 110.6 %all-reduce.3.cloned.1.call-done = (f32[512,512]{0,1:T(8,128)}, f32[512,512]{0,1:T(8,128)}) async-done(((f32[512,512]{0,1:T(8,128)}, f32[512,512]{0,1:T(8,128)}), (f32[512,512]{0,1:T(8,128)}, f32[512,512]{0,1:T(8,128)})) %all-reduce.3.cloned.1.call-update) | async-done | bytes 2097168 | tf_op jit(solution)/shard_map/psum | solution.py:65
  262.8 1.8 broadcast_multiply_fusion
  264.5 1.3 copy.15
  265.9 1.3 copy.16
  (35 shorter events, 1.8 us)
Async XLA Ops:
  7.2 26.4 %copy-start = (bf16[512,512]{1,0:T(8,128)(2,1)S(1)}, bf16[512,512]{1,0:T(8,128)(2,1)}, u32[]{:S(2)}) copy-start(bf16[512,512]{1,0:T(8,128)(2,1)} %param.14) | copy-start | bytes 1572868
  7.2 13.1 %copy-start.2 = (bf16[256,512]{1,0:T(8,128)(2,1)S(1)}, bf16[256,512]{1,0:T(8,128)(2,1)}, u32[]{:S(2)}) copy-start(bf16[256,512]{1,0:T(8,128)(2,1)} %param.9) | copy-start | bytes 786436
  7.2 255.6 %all-reduce.3.cloned.1.call-start = ((), (), s32[]{:S(2)}) async-start(), calls=%async_computation | async-start | bytes 4194304 | tf_op jit(solution)/shard_map/psum | solution.py:65
  7.2 11.5 %collective-permute-start = (bf16[2,128,512]{2,1,0:T(8,128)(2,1)}, bf16[2,128,512]{2,1,0:T(8,128)(2,1)S(1)}, u32[]{:S(2)}, u32[]{:S(2)}) collective-permute-start(bf16[2,128,512]{2,1,0:T(8,128)(2,1)} %bitcast.67), channel_id=1, source_target_pairs={{0,2},{1,3},{2,4},{3,5},{4,6},{5,7},{6,0},{7,1},{8,10},{9,11},{10,... | collective-permute-start | bytes 786440 | tf_op jit(solution)/shard_map/ppermute | solution.py:13
  9.3 10.9 %collective-permute-start.1 = (bf16[2,128,512]{2,1,0:T(8,128)(2,1)}, bf16[2,128,512]{2,1,0:T(8,128)(2,1)S(1)}, u32[]{:S(2)}, u32[]{:S(2)}) collective-permute-start(bf16[2,128,512]{2,1,0:T(8,128)(2,1)} %bitcast.68), channel_id=1, source_target_pairs={{0,1},{1,2},{2,3},{3,4},{4,5},{5,6},{6,7},{7,0},{8,9},{9,10},{10,1... | collective-permute-start | bytes 786440 | tf_op jit(solution)/shard_map/ppermute | solution.py:13
  11.4 12.7 %collective-permute-start.2 = (bf16[2,128,512]{2,1,0:T(8,128)(2,1)}, bf16[2,128,512]{2,1,0:T(8,128)(2,1)S(1)}, u32[]{:S(2)}, u32[]{:S(2)}) collective-permute-start(bf16[2,128,512]{2,1,0:T(8,128)(2,1)} %bitcast.69), channel_id=1, source_target_pairs={{0,7},{1,0},{2,1},{3,2},{4,3},{5,4},{6,5},{7,6},{8,15},{9,8},{10,9... | collective-permute-start | bytes 786440 | tf_op jit(solution)/shard_map/ppermute | solution.py:13
  11.4 16.3 %collective-permute-start.3 = (bf16[2,128,512]{2,1,0:T(8,128)(2,1)}, bf16[2,128,512]{2,1,0:T(8,128)(2,1)S(1)}, u32[]{:S(2)}, u32[]{:S(2)}) collective-permute-start(bf16[2,128,512]{2,1,0:T(8,128)(2,1)} %bitcast.70), channel_id=1, source_target_pairs={{0,6},{1,7},{2,0},{3,1},{4,2},{5,3},{6,4},{7,5},{8,14},{9,15},{10,... | collective-permute-start | bytes 786440 | tf_op jit(solution)/shard_map/ppermute | solution.py:13
  27.7 2.8 %copy-start.1 = (bf16[2,16,128,128]{3,2,1,0:T(8,128)(2,1)S(1)}, bf16[2,16,128,128]{3,2,1,0:T(8,128)(2,1)}, u32[]{:S(2)}) copy-start(bf16[2,16,128,128]{3,2,1,0:T(8,128)(2,1)} %param.10) | copy-start | bytes 3145732
  30.5 3.1 %copy-start.4 = (f32[256,512]{1,0:T(8,128)S(1)}, f32[256,512]{1,0:T(8,128)}, u32[]{:S(2)}) copy-start(f32[256,512]{1,0:T(8,128)} %fusion.33) | copy-start | bytes 1572868
  30.5 3.1 %copy-start.5 = (bf16[256,512]{1,0:T(8,128)(2,1)S(1)}, bf16[256,512]{1,0:T(8,128)(2,1)}, u32[]{:S(2)}) copy-start(bf16[256,512]{1,0:T(8,128)(2,1)} %param.17) | copy-start | bytes 786436
  128.8 22.3 %copy-start.3 = (bf16[512,512]{1,0:T(8,128)(2,1)S(1)}, bf16[512,512]{1,0:T(8,128)(2,1)}, u32[]{:S(2)}) copy-start(bf16[512,512]{1,0:T(8,128)(2,1)} %param.13) | copy-start | bytes 1572868
  128.9 6.4 %collective-permute-start.4 = (bf16[2,128,512]{2,1,0:T(8,128)(2,1)S(1)}, bf16[2,128,512]{2,1,0:T(8,128)(2,1)S(1)}, u32[]{:S(2)}, u32[]{:S(2)}) collective-permute-start(bf16[2,128,512]{2,1,0:T(8,128)(2,1)S(1)} %bitcast.78), channel_id=1, source_target_pairs={{0,6},{1,7},{2,0},{3,1},{4,2},{5,3},{6,4},{7,5},{8,14},{9,15},{10,... | collective-permute-start | bytes 786440 | tf_op jit(solution)/shard_map/ppermute | solution.py:13
  130.2 17.8 %collective-permute-start.5 = (bf16[2,128,512]{2,1,0:T(8,128)(2,1)S(1)}, bf16[2,128,512]{2,1,0:T(8,128)(2,1)S(1)}, u32[]{:S(2)}, u32[]{:S(2)}) collective-permute-start(bf16[2,128,512]{2,1,0:T(8,128)(2,1)S(1)} %bitcast.79), channel_id=1, source_target_pairs={{0,7},{1,0},{2,1},{3,2},{4,3},{5,4},{6,5},{7,6},{8,15},{9,8},{10,9... | collective-permute-start | bytes 786440 | tf_op jit(solution)/shard_map/ppermute | solution.py:13
  132.1 15.9 %collective-permute-start.6 = (bf16[2,128,512]{2,1,0:T(8,128)(2,1)S(1)}, bf16[2,128,512]{2,1,0:T(8,128)(2,1)S(1)}, u32[]{:S(2)}, u32[]{:S(2)}) collective-permute-start(bf16[2,128,512]{2,1,0:T(8,128)(2,1)S(1)} %bitcast.80), channel_id=1, source_target_pairs={{0,1},{1,2},{2,3},{3,4},{4,5},{5,6},{6,7},{7,0},{8,9},{9,10},{10,1... | collective-permute-start | bytes 786440 | tf_op jit(solution)/shard_map/ppermute | solution.py:13
  132.2 18.7 %collective-permute-start.7 = (bf16[2,128,512]{2,1,0:T(8,128)(2,1)S(1)}, bf16[2,128,512]{2,1,0:T(8,128)(2,1)S(1)}, u32[]{:S(2)}, u32[]{:S(2)}) collective-permute-start(bf16[2,128,512]{2,1,0:T(8,128)(2,1)S(1)} %bitcast.81), channel_id=1, source_target_pairs={{0,2},{1,3},{2,4},{3,5},{4,6},{5,7},{6,0},{7,1},{8,10},{9,11},{10,... | collective-permute-start | bytes 786440 | tf_op jit(solution)/shard_map/ppermute | solution.py:13
Sparse Core Ops, SparseCore 0:
  128.1 134.5 all-reduce.2
where the time goes:
time: 276 us; the launch traced here: 274 us
  waiting for transfers between devices  136 us (49%)
  other arithmetic  85 us (31%)
  local copies, waits for them, and re-layouts  16.1 us (6%)
  between operations  14.2 us (5%)
  matrix products  11.9 us (4%)
  starting transfers between devices  10.6 us (4%)
    psum x1, waiting for transfers between devices, local(): total_self, total_neigh = lax.psum((part_self, part_neigh), ('grp', 'feat'))  111 us
    scatter-add x1, other arithmetic, local(): jax.ops.segment_sum(contrib_flat, flat_index, num_segments=window_count)  76 us
    ppermute x8, waiting for transfers between devices, passed_along(): return lax.ppermute(x, axis, [(i, (i + by) % peers) for i in range(peers)])  25.7 us
    unnamed x23, local copies, waits for them, and re-layouts  10.9 us
    ppermute x8, starting transfers between devices, passed_along(): return lax.ppermute(x, axis, [(i, (i + by) % peers) for i in range(peers)])  10.5 us
  transfers between devices with their start and end apart: 9, of which 7 were waited for; matrix products, arithmetic and copies ran while one was open for 3% of the time, Pallas kernels for 0%

commit v1 on v0

v1 whole, which is shorter than its diff:
```python
import functools
import math

import jax
import jax.numpy as jnp
from jax import lax
from jax.experimental import pallas as pl
from jax.experimental.pallas import tpu as pltpu
from jax.sharding import PartitionSpec as P

SPAN = 2
WIN = 2 * SPAN + 1
MESH = pl.DeviceIdType.MESH
LANES = 128
STRIP = 32


def dot_nn(a, b):
    return jnp.dot(a, b, preferred_element_type=jnp.float32)


def dot_tn(a, b):
    return lax.dot_general(a, b, (((0,), (0,)), ((), ())), preferred_element_type=jnp.float32)


def dot_nt(a, b):
    return lax.dot_general(a, b, (((1,), (1,)), ((), ())), preferred_element_type=jnp.float32)


def strips(rows, body, step=STRIP):
    def run(i, carry):
        body(pl.ds(pl.multiple_of(i * step, step), step))
        return carry

    lax.fori_loop(0, rows // step, run, 0)


def kernel(
    n_feat, n_grp,
    src_ref, cnt_ref, feat_ref, adj_ref, ws_ref, wn_ref, scale_ref, cot_ref,
    out_ref, gfeat_ref, grads_ref,
    pool, dense, dsum, inv, summed, preact, both, gpre,
    part_out, part_own, part_in, buf1, in2, buf2, in3, full,
    back, term_out, term_sum, term_in,
    halo_s, halo_r, term_s, term_r,
    rs1_s, rs1_r, rs2_s, rs2_r, rs3_s, rs3_r,
    ag1_s, ag1_r, ag2_s, ag2_r, ag3_s, ag3_r,
):
    n_chip = n_feat // 2
    me = lax.axis_index("feat")
    grp = lax.axis_index("grp")
    core = lax.rem(me, 2)
    chip = me // 2
    partner = me + 1 - 2 * core
    num_blocks, num_slots, block_len, _ = adj_ref.shape
    rows, width = feat_ref.shape
    ahead = lax.rem(me + 2, n_feat)
    behind = lax.rem(me + n_feat - 2, n_feat)
    chip_peers = [2 * lax.rem(chip + j, n_chip) + core for j in range(1, n_chip)]
    grp_peers = [lax.rem(grp + j, n_grp) for j in range(1, n_grp)]

    def to_feat(peer):
        return (grp, peer)

    def to_grp(peer):
        return (peer, me)

    def send(src, dst, ssem, rsem, device):
        copy = pltpu.make_async_remote_copy(
            src_ref=src, dst_ref=dst, send_sem=ssem, recv_sem=rsem, device_id=device, device_id_type=MESH
        )
        copy.start()
        return copy

    def landed(dst, rsem):
        pltpu.make_async_remote_copy(
            src_ref=dst, dst_ref=dst, send_sem=rsem, recv_sem=rsem, device_id=to_feat(partner), device_id_type=MESH
        ).wait_recv()

    sent = []

    barrier = pltpu.get_barrier_semaphore()
    partners = [to_feat(partner)] + [to_feat(p) for p in chip_peers] + [to_grp(p) for p in grp_peers]
    for device in partners:
        pl.semaphore_signal(barrier, inc=1, device_id=device, device_id_type=MESH)
    pl.semaphore_wait(barrier, len(partners))

    sent.append(send(feat_ref, pool.at[0], halo_s.at[0], halo_r.at[0], to_feat(ahead)))
    sent.append(send(feat_ref, pool.at[4], halo_s.at[1], halo_r.at[4], to_feat(behind)))
    near = 3 - 2 * core
    passed = 1 + 2 * core
    sent.append(send(feat_ref, pool.at[passed], halo_s.at[2], halo_r.at[passed], to_feat(partner)))

    dsum[...] = jnp.zeros_like(dsum)

    def build(piece, carry):
        owner = lax.rem(me + piece - SPAN + n_feat, n_feat)
        for b in range(num_blocks):
            dst_rows = slice(b * block_len, (b + 1) * block_len)
            for h in range(num_blocks):
                source = owner * num_blocks + h
                acc = jnp.zeros((block_len, block_len), jnp.float32)
                for k in range(num_slots):
                    hit = jnp.logical_and(src_ref[b, k] == source, cnt_ref[b] > k)
                    acc = acc + adj_ref[b, k].astype(jnp.float32) * jnp.where(hit, 1.0, 0.0)
                dsum[dst_rows, :] += acc
                dense[piece, dst_rows, h * block_len : (h + 1) * block_len] = acc.astype(jnp.bfloat16)
        return carry

    lax.fori_loop(0, WIN, build, 0)
    inv[...] = jnp.broadcast_to(lax.rsqrt(jnp.sum(dsum[...], axis=1, keepdims=True)), inv.shape)
    both[0] = feat_ref[...]
    preact[...] = dot_nn(feat_ref[...], ws_ref[...])
    summed[...] = dot_nn(dense[SPAN], feat_ref[...])

    landed(pool.at[near], halo_r.at[near])
    summed[...] += dot_nn(dense[near], pool[near])
    far = 4 - 4 * core
    landed(pool.at[far], halo_r.at[far])
    sent.append(send(pool.at[far], pool.at[near], halo_s.at[3], halo_r.at[near], to_feat(partner)))
    summed[...] += dot_nn(dense[far], pool[far])
    other = 4 * core
    landed(pool.at[other], halo_r.at[other])
    summed[...] += dot_nn(dense[other], pool[other])
    landed(pool.at[passed], halo_r.at[passed])
    summed[...] += dot_nn(dense[passed], pool[passed])

    def aggregate(at):
        both[1, at, :] = (summed[at, :] * inv[at, :1]).astype(jnp.bfloat16)

    strips(rows, aggregate)
    preact[...] += dot_nn(both[1], wn_ref[...])

    def activate(at):
        scale = scale_ref[...]
        scaled = preact[at, :] * scale
        gate = 1.0 / (1.0 + jnp.exp(-scaled))
        out_ref[at, :] = (scaled * gate).astype(jnp.bfloat16)
        gpre[at, :] = (
            cot_ref[at, :].astype(jnp.float32) * gate * (1.0 + scaled * (1.0 - gate)) * scale
        ).astype(jnp.bfloat16)

    strips(rows, activate)

    panels = width // LANES
    given = dot_tn(both[1 - core], gpre[...])
    for j in range(panels):
        part_out[j * width : (j + 1) * width, :] = given[:, j * LANES : (j + 1) * LANES].astype(jnp.bfloat16)
    sent.append(send(part_out, part_in, rs1_s, rs1_r, to_feat(partner)))
    kept = dot_tn(both[core], gpre[...])
    for j in range(panels):
        part_own[j * width : (j + 1) * width, :] = kept[:, j * LANES : (j + 1) * LANES]

    pulled = dot_nt(gpre[...], wn_ref[...])
    back[...] = (pulled * inv[:, :1]).astype(jnp.bfloat16)
    term_out[passed] = dot_tn(dense[passed], back[...]).astype(jnp.bfloat16)
    sent.append(send(term_out.at[passed], term_in.at[2], term_s.at[0], term_r.at[2], to_feat(partner)))

    landed(part_in, rs1_r)

    def merge1(at):
        buf1[at, :] = (part_own[at, :] + part_in[at, :].astype(jnp.float32)).astype(jnp.bfloat16)

    strips(buf1.shape[0], merge1, 128)
    c2 = buf2.shape[0]
    c3 = c2 // n_grp
    for j, peer in enumerate(chip_peers):
        at = pl.ds(pl.multiple_of((peer // 2) * c2, c2), c2)
        sent.append(send(buf1.at[at], in2.at[j], rs2_s.at[j], rs2_r.at[j], to_feat(peer)))

    term_out[other] = dot_tn(dense[other], back[...]).astype(jnp.bfloat16)
    sent.append(
        send(term_out.at[other], term_in.at[far], term_s.at[1], term_r.at[far], to_feat(lax.rem(me + other - 2 + n_feat, n_feat)))
    )
    term_sum[...] = dot_tn(dense[far], back[...])
    landed(term_in.at[2], term_r.at[2])
    term_out[far] = (term_sum[...] + term_in[2].astype(jnp.float32)).astype(jnp.bfloat16)
    sent.append(
        send(term_out.at[far], term_in.at[other], term_s.at[2], term_r.at[other], to_feat(lax.rem(me + far - 2 + n_feat, n_feat)))
    )
    term_out[near] = dot_tn(dense[near], back[...]).astype(jnp.bfloat16)
    sent.append(send(term_out.at[near], term_in.at[passed], term_s.at[3], term_r.at[passed], to_feat(partner)))
    term_sum[...] = dot_nt(gpre[...], ws_ref[...])
    term_sum[...] += dot_tn(dense[SPAN], back[...])

    for j in range(n_chip - 1):
        landed(in2.at[j], rs2_r.at[j])
    mine2 = chip * c2

    def merge2(at):
        total = buf1[pl.ds(pl.multiple_of(mine2 + at.start, 16), at.size), :].astype(jnp.float32)
        for j in range(n_chip - 1):
            total = total + in2[j, at, :].astype(jnp.float32)
        buf2[at, :] = total.astype(jnp.bfloat16)

    strips(c2, merge2, min(c2, 128))
    for j, peer in enumerate(grp_peers):
        at = pl.ds(pl.multiple_of(peer * c3, c3), c3)
        sent.append(send(buf2.at[at], in3.at[j], rs3_s.at[j], rs3_r.at[j], to_grp(peer)))
    for j in range(n_grp - 1):
        landed(in3.at[j], rs3_r.at[j])
    total = buf2[pl.ds(pl.multiple_of(grp * c3, c3), c3), :].astype(jnp.float32)
    for j in range(n_grp - 1):
        total = total + in3[j].astype(jnp.float32)
    half = buf1.shape[0]

    def piece3(owner):
        return pl.ds(pl.multiple_of(core * half + chip * c2 + owner * c3, c3), c3)

    def piece2(owner):
        return pl.ds(pl.multiple_of(core * half + owner * c2, c2), c2)

    def piece1(owner):
        return pl.ds(pl.multiple_of(owner * half, half), half)

    full[piece3(grp), :] = total.astype(jnp.bfloat16)
    for j, peer in enumerate(grp_peers):
        place = full.at[piece3(grp)]
        sent.append(send(place, place, ag3_s.at[j], ag3_r.at[j], to_grp(peer)))
    for j in range(n_grp - 1):
        landed(full.at[piece3(lax.rem(grp + n_grp - 1 - j, n_grp))], ag3_r.at[j])
    for j, peer in enumerate(chip_peers):
        place = full.at[piece2(chip)]
        sent.append(send(place, place, ag2_s.at[j], ag2_r.at[j], to_feat(peer)))

    for slot in (near, other, far):
        landed(term_in.at[slot], term_r.at[slot])

    def finish(at):
        grad = term_sum[at, :]
        for slot in (near, other, far):
            grad = grad + term_in[slot, at, :].astype(jnp.float32)
        gfeat_ref[at, :] = grad.astype(jnp.bfloat16)

    strips(rows, finish)

    for j in range(n_chip - 1):
        landed(full.at[piece2(lax.rem(chip + n_chip - 1 - j, n_chip))], ag2_r.at[j])
    place = full.at[piece1(core)]
    sent.append(send(place, place, ag1_s, ag1_r, to_feat(partner)))
    landed(full.at[piece1(1 - core)], ag1_r)
    grads_ref[...] = full[...]
    for copy in sent:
        copy.wait_send()


def local(
    n_feat, n_grp, features, adj_tiles, src_block, counts, w_self, w_neigh, multiplier, bit_shift, cotangent
):
    rows, width = features.shape
    hidden = w_self.shape[1]
    scale = (multiplier * jnp.exp2(-bit_shift.astype(jnp.float32)))[None, :]
    n_chip = n_feat // 2
    half = width * hidden // LANES
    c2 = half // n_chip
    c3 = c2 // n_grp
    bf, f32 = jnp.bfloat16, jnp.float32
    vmem = pl.BlockSpec(memory_space=pltpu.VMEM)
    smem = pl.BlockSpec(memory_space=pltpu.SMEM)
    dma = pltpu.SemaphoreType.DMA
    output, grad_features, grads = pl.pallas_call(
        functools.partial(kernel, n_feat, n_grp),
        out_shape=(
            jax.ShapeDtypeStruct((rows, hidden), bf),
            jax.ShapeDtypeStruct((rows, width), bf),
            jax.ShapeDtypeStruct((2 * half, LANES), bf),
        ),
        in_specs=[smem, smem] + [vmem] * 6,
        out_specs=(vmem, vmem, vmem),
        scratch_shapes=[
            pltpu.VMEM((WIN, rows, width), bf),
            pltpu.VMEM((WIN, rows, rows), bf),
            pltpu.VMEM((rows, adj_tiles.shape[3]), f32),
            pltpu.VMEM((rows, LANES), f32),
            pltpu.VMEM((rows, width), f32),
            pltpu.VMEM((rows, hidden), f32),
            pltpu.VMEM((2, rows, width), bf),
            pltpu.VMEM((rows, hidden), bf),
            pltpu.VMEM((half, LANES), bf),
            pltpu.VMEM((half, LANES), f32),
            pltpu.VMEM((half, LANES), bf),
            pltpu.VMEM((half, LANES), bf),
            pltpu.VMEM((n_chip - 1, c2, LANES), bf),
            pltpu.VMEM((c2, LANES), bf),
            pltpu.VMEM((n_grp - 1, c3, LANES), bf),
            pltpu.VMEM((2 * half, LANES), bf),
            pltpu.VMEM((rows, width), bf),
            pltpu.VMEM((WIN, rows, width), bf),
            pltpu.VMEM((rows, width), f32),
            pltpu.VMEM((WIN, rows, width), bf),
            dma((4,)), dma((WIN,)), dma((4,)), dma((WIN,)),
            dma, dma, dma((n_chip - 1,)), dma((n_chip - 1,)), dma((n_grp - 1,)), dma((n_grp - 1,)),
            dma, dma, dma((n_chip - 1,)), dma((n_chip - 1,)), dma((n_grp - 1,)), dma((n_grp - 1,)),
        ],
        compiler_params=pltpu.CompilerParams(
            collective_id=0, has_side_effects=True, vmem_limit_bytes=48 * 1024 * 1024
        ),
    )(src_block, counts, features, adj_tiles, w_self, w_neigh, scale, cotangent)
    grad_scale = 1.0 / math.sqrt(rows * n_grp * n_feat)
    grads = grads.reshape(2, hidden // LANES, width, LANES).transpose(0, 2, 1, 3).reshape(2, width, hidden)
    return (output, grad_features, grads[0].astype(f32) * grad_scale, grads[1].astype(f32) * grad_scale)


def solution(mesh):
    return jax.shard_map(
        functools.partial(local, mesh.shape["feat"], mesh.shape["grp"]),
        mesh=mesh,
        in_specs=(
            P(("grp", "feat"), None),
            P(("grp", "feat"), None, None, None),
            P(("grp", "feat"), None),
            P(("grp", "feat")),
            P(),
            P(),
            P(),
            P(),
            P(("grp", "feat"), None),
        ),
        out_specs=(P(("grp", "feat"), None), P(("grp", "feat"), None), P(), P()),
        check_vma=False,
    )
```

time: 276 us -> 61.8 us (0.22)
  waiting for transfers between devices: 136 us -> 0 us
  other arithmetic: 85 us -> 0.88 us
  Pallas kernels: 0 us -> 49.8 us
  between operations: 14.2 us -> 0.67 us
  matrix products: 11.9 us -> 0 us
  starting transfers between devices: 10.6 us -> 0 us
  local copies, waits for them, and re-layouts: 16.1 us -> 10.1 us
    psum x1 -> x0, waiting for transfers between devices: 111 us -> none  [local(): total_self, total_neigh = lax.psum((part_self, part_neigh), ('grp', 'feat'))]
    scatter-add x1 -> x0, other arithmetic: 76 us -> none  [local(): jax.ops.segment_sum(contrib_flat, flat_index, num_segments=window_count)]
    pallas_call x0 -> x1, Pallas kernels: none -> 49.8 us  [local(): pl.pallas_call(functools.partial(kernel, n_feat, n_grp), out_shape=(jax.S...]
    ppermute x8 -> x0, waiting for transfers between devices: 25.7 us -> none  [passed_along(): return lax.ppermute(x, axis, [(i, (i + by) % peers) for i in range(peers)])]
    dot_general x8 -> x0, matrix products: 11.9 us -> none  [the longest x1 3.1 us: local(): jnp.einsum('bkij,bkjf->bif', masked, sources, preferred_element_type=jnp....]
    ppermute x8 -> x0, starting transfers between devices: 10.5 us -> none  [passed_along(): return lax.ppermute(x, axis, [(i, (i + by) % peers) for i in range(peers)])]
    unnamed x23 -> x16, local copies, waits for them, and re-layouts: 10.9 us -> 7.29 us
    mul x0 -> x3, local copies, waits for them, and re-layouts: none -> 2.84 us  [the longest x2 2.16 us: local(): grads[1].astype(f32) * grad_scale]
  transfers between devices with their start and end apart: 9 -> 0, of which waited for: 7 -> 0; matrix products, arithmetic and copies ran while one was open for 3% -> 0% of each run, Pallas kernels for 0% -> 0%
where the time goes in v1:
time: 61.8 us; the launch traced here: 61.5 us
  Pallas kernels  49.8 us (81%)
  local copies, waits for them, and re-layouts  10.1 us (16%)
  other arithmetic  0.88 us (1%)
  between operations  0.67 us (1%)
    pallas_call x1, Pallas kernels, local(): pl.pallas_call(functools.partial(kernel, n_feat, n_grp), out_shape=(jax.S...  49.8 us
    unnamed x16, local copies, waits for them, and re-layouts  7.29 us
    mul x2, local copies, waits for them, and re-layouts, local(): grads[1].astype(f32) * grad_scale  2.16 us

profile of v1, /device:TPU:1, one launch (start us, length us, event | category | flops | bytes accessed | tf_op | source)
XLA Modules:
  0.0 61.5 jit_solution(10373093406830124763)
XLA Ops:
  0.6 0.7 %exponential_multiply_fusion = f32[512]{0:T(512)S(1)} fusion(f32[512]{0:T(512)} %param.15, s32[512]{0:T(512)} %param.16), kind=kLoop, calls=%fused_computation.4 | loop fusion | flops 2048 | bytes 6144 | tf_op jit(solution)/shard_map/mul | solution.py:252
  1.3 0.0 copy-start.5
  1.3 0.0 copy-start.6
  1.3 0.7 %copy-done.5 = s32[2,16]{1,0:T(2,128)S(1)} copy-done((s32[2,16]{1,0:T(2,128)S(1)}, s32[2,16]{1,0:T(2,128)}, u32[]{:S(2)}) %copy-start.5) | copy-done | bytes 152
  2.0 0.0 copy-done.6
  2.0 0.0 copy-start
  2.0 1.2 %copy-done = bf16[2,16,128,128]{3,2,1,0:T(8,128)(2,1)S(1)} copy-done((bf16[2,16,128,128]{3,2,1,0:T(8,128)(2,1)S(1)}, bf16[2,16,128,128]{3,2,1,0:T(8,128)(2,1)}, u32[]{:S(2)}) %copy-start) | copy-done | bytes 1048600
  3.2 0.0 copy-start.1
  3.3 1.0 %copy-done.1 = bf16[512,512]{1,0:T(8,128)(2,1)S(1)} copy-done((bf16[512,512]{1,0:T(8,128)(2,1)S(1)}, bf16[512,512]{1,0:T(8,128)(2,1)}, u32[]{:S(2)}) %copy-start.1) | copy-done | bytes 524312
  4.3 0.0 copy-start.2
  4.3 1.0 %copy-done.2 = bf16[512,512]{1,0:T(8,128)(2,1)S(1)} copy-done((bf16[512,512]{1,0:T(8,128)(2,1)S(1)}, bf16[512,512]{1,0:T(8,128)(2,1)}, u32[]{:S(2)}) %copy-start.2) | copy-done | bytes 524312
  5.3 0.0 copy-start.3
  5.3 0.9 %copy-done.3 = bf16[256,512]{1,0:T(8,128)(2,1)S(1)} copy-done((bf16[256,512]{1,0:T(8,128)(2,1)S(1)}, bf16[256,512]{1,0:T(8,128)(2,1)}, u32[]{:S(2)}) %copy-start.3) | copy-done | bytes 262168
  6.3 0.0 copy-start.4
  6.3 0.9 %copy-done.4 = bf16[256,512]{1,0:T(8,128)(2,1)S(1)} copy-done((bf16[256,512]{1,0:T(8,128)(2,1)S(1)}, bf16[256,512]{1,0:T(8,128)(2,1)}, u32[]{:S(2)}) %copy-start.4) | copy-done | bytes 262168
  7.2 49.8 %shard_map.120 = (bf16[256,512]{1,0:T(8,128)(2,1)S(1)}, bf16[256,512]{1,0:T(8,128)(2,1)S(1)}, bf16[4096,128]{1,0:T(8,128)(2,1)S(1)}) custom-call(s32[2,16]{1,0:T(2,128)S(1)} %copy-done.5, s32[2]{0:T(128)S(1)} %copy-done.6, bf16[256,512]{1,0:T(8,128)(2,1)S(1)} %copy-done.3, bf16[2,16,128,128]{3,2,1,0:T(8,128)(2,1)S(1)} %copy-done, ...), custom_call_target="tpu_custom_call" | custom-call | tf_op jit(solution)/shard_map/pallas_call | solution.py:261
  57.0 0.2 convert_multiply_fusion
  57.2 0.7 %copy.14 = f32[1,512,4,128]{3,2,1,0:T(4,128)S(1)} copy(f32[1,512,4,128]{3,1,2,0:T(8,128)S(1)} %get-tuple-element.10) | data formatting | bytes 2097152 | tf_op jit(solution)/shard_map/mul | solution.py:301
  57.9 0.7 %copy.13 = f32[1,512,4,128]{3,2,1,0:T(4,128)S(1)} copy(f32[1,512,4,128]{3,1,2,0:T(8,128)S(1)} %get-tuple-element.11) | data formatting | bytes 2097152 | tf_op jit(solution)/shard_map/mul | solution.py:301
  58.6 1.5 %copy_bitcast_fusion = (f32[512,512]{1,0:T(8,128)}, f32[512,512]{1,0:T(8,128)}) fusion(f32[64,8,4,128]{3,2,1,0:T(4,128)S(1)} %bitcast.14, f32[64,8,4,128]{3,2,1,0:T(4,128)S(1)} %bitcast.15), kind=kLoop, calls=%fused_computation | loop fusion | bytes 4194304 | tf_op jit(solution)/shard_map/mul | solution.py:301
  60.1 0.7 %copy.21 = bf16[256,512]{1,0:T(8,128)(2,1)} copy(bf16[256,512]{1,0:T(8,128)(2,1)S(1)} %get-tuple-element.18) | data formatting | bytes 524288
  60.8 0.7 %copy.22 = bf16[256,512]{1,0:T(8,128)(2,1)} copy(bf16[256,512]{1,0:T(8,128)(2,1)S(1)} %get-tuple-element.19) | data formatting | bytes 524288
Async XLA Ops:
  1.3 0.7 %copy-start.5 = (s32[2,16]{1,0:T(2,128)S(1)}, s32[2,16]{1,0:T(2,128)}, u32[]{:S(2)}) copy-start(s32[2,16]{1,0:T(2,128)} %src_ref.1) | copy-start | bytes 388
  1.3 0.7 %copy-start.6 = (s32[2]{0:T(128)S(1)}, s32[2]{0:T(128)}, u32[]{:S(2)}) copy-start(s32[2]{0:T(128)} %cnt_ref.1) | copy-start | bytes 28
  2.0 1.2 %copy-start = (bf16[2,16,128,128]{3,2,1,0:T(8,128)(2,1)S(1)}, bf16[2,16,128,128]{3,2,1,0:T(8,128)(2,1)}, u32[]{:S(2)}) copy-start(bf16[2,16,128,128]{3,2,1,0:T(8,128)(2,1)} %adj_ref.1) | copy-start | bytes 3145732
  3.2 1.0 %copy-start.1 = (bf16[512,512]{1,0:T(8,128)(2,1)S(1)}, bf16[512,512]{1,0:T(8,128)(2,1)}, u32[]{:S(2)}) copy-start(bf16[512,512]{1,0:T(8,128)(2,1)} %ws_ref.1) | copy-start | bytes 1572868
  4.3 1.0 %copy-start.2 = (bf16[512,512]{1,0:T(8,128)(2,1)S(1)}, bf16[512,512]{1,0:T(8,128)(2,1)}, u32[]{:S(2)}) copy-start(bf16[512,512]{1,0:T(8,128)(2,1)} %wn_ref.1) | copy-start | bytes 1572868
  5.3 0.9 %copy-start.3 = (bf16[256,512]{1,0:T(8,128)(2,1)S(1)}, bf16[256,512]{1,0:T(8,128)(2,1)}, u32[]{:S(2)}) copy-start(bf16[256,512]{1,0:T(8,128)(2,1)} %feat_ref.1) | copy-start | bytes 786436
  6.3 0.9 %copy-start.4 = (bf16[256,512]{1,0:T(8,128)(2,1)S(1)}, bf16[256,512]{1,0:T(8,128)(2,1)}, u32[]{:S(2)}) copy-start(bf16[256,512]{1,0:T(8,128)(2,1)} %cot_ref.1) | copy-start | bytes 786436

commit v2 on v1

v2 whole, which is shorter than its diff:
```python
import functools
import math

import jax
import jax.numpy as jnp
from jax import lax
from jax.experimental import pallas as pl
from jax.experimental.pallas import tpu as pltpu
from jax.sharding import PartitionSpec as P

SPAN = 2
WIN = 2 * SPAN + 1
MESH = pl.DeviceIdType.MESH
STRIP = 32
CHUNKS = 4
SPARE = 1
SPLIT = 3


def dot_nn(a, b):
    return jnp.dot(a, b, preferred_element_type=jnp.float32)


def dot_tn(a, b):
    return lax.dot_general(a, b, (((0,), (0,)), ((), ())), preferred_element_type=jnp.float32)


def dot_nt(a, b):
    return lax.dot_general(a, b, (((1,), (1,)), ((), ())), preferred_element_type=jnp.float32)


def strips(rows, body, step=STRIP):
    def run(i, carry):
        body(pl.ds(pl.multiple_of(i * step, step), step))
        return carry

    lax.fori_loop(0, rows // step, run, 0)


def kernel(
    n_feat, n_grp, fine,
    src_ref, cnt_ref, feat_hbm, adj_hbm, ws_hbm, wn_hbm, mult_hbm, shift_hbm, cot_hbm,
    out_hbm, gfeat_hbm, grads_hbm,
    out_ref, gfeat_ref,
    adj_ref, ws_ref, wn_ref, mult_ref, shift_ref, cot_ref,
    pool, dense, dsum, inv, summed, preact, both, gpre,
    part_out, part_own, part_in, buf1, in2, buf2, in3, full,
    back, term_out, term_sum, own_grad, term_in,
    load_s, store_s, halo_s, halo_r, term_s, term_r,
    rs1_s, rs1_r, rs2_s, rs2_r, rs3_s, rs3_r,
    ag1_s, ag1_r, ag2_s, ag2_r, ag3_s, ag3_r,
):
    n_chip = n_feat // 2
    square = n_chip == 4
    me = lax.axis_index("feat")
    grp = lax.axis_index("grp")
    core = lax.rem(me, 2)
    chip = me // 2
    odd = lax.rem(chip, 2)
    partner = me + 1 - 2 * core
    num_blocks, num_slots, block_len, _ = adj_ref.shape
    rows, width = feat_hbm.shape
    lanes = buf1.shape[1]
    ahead = lax.rem(me + 2, n_feat)
    behind = lax.rem(me + n_feat - 2, n_feat)
    chip_peers = [2 * lax.rem(chip + j, n_chip) + core for j in range(1, n_chip)]
    grp_peers = [lax.rem(grp + j, n_grp) for j in range(1, n_grp)]
    x_slot = 4 - 4 * odd
    y_slot = 4 * odd
    x_peer = 2 * (chip + 1 - 2 * odd) + core
    y_peer = 2 * lax.rem(chip + 2, n_chip) + core

    def to_feat(peer):
        return (grp, peer)

    def to_grp(peer):
        return (peer, me)

    sent = []

    def send(src, dst, ssem, rsem, device):
        copy = pltpu.make_async_remote_copy(
            src_ref=src, dst_ref=dst, send_sem=ssem, recv_sem=rsem, device_id=device, device_id_type=MESH
        )
        copy.start()
        sent.append(copy)

    def landed(dst, rsem):
        pltpu.make_async_remote_copy(
            src_ref=dst, dst_ref=dst, send_sem=rsem, recv_sem=rsem, device_id=to_feat(partner), device_id_type=MESH
        ).wait_recv()

    loads = [
        pltpu.make_async_copy(src, dst, load_s.at[i])
        for i, (src, dst) in enumerate(
            (
                (adj_hbm, adj_ref), (feat_hbm, both.at[0]), (ws_hbm, ws_ref), (wn_hbm, wn_ref),
                (mult_hbm, mult_ref), (shift_hbm, shift_ref), (cot_hbm, cot_ref),
            )
        )
    ]
    for load in loads:
        load.start()

    barrier = pltpu.get_barrier_semaphore()
    partners = [to_feat(partner)] + [to_feat(p) for p in chip_peers] + [to_grp(p) for p in grp_peers]
    for device in partners:
        pl.semaphore_signal(barrier, inc=1, device_id=device, device_id_type=MESH)
    pl.semaphore_wait(barrier, len(partners))

    near = 3 - 2 * core
    passed = 1 + 2 * core
    far = 4 - 4 * core
    other = 4 * core
    step = rows // CHUNKS
    chunks = [pl.ds(c * step, step) for c in range(CHUNKS)]
    if square:
        for c, at in enumerate(chunks):
            send(feat_hbm.at[at], pool.at[y_slot, at], halo_s.at[0, c], halo_r.at[y_slot, c], to_feat(x_peer))
    else:
        for c, at in enumerate(chunks):
            send(feat_hbm.at[at], pool.at[0, at], halo_s.at[0, c], halo_r.at[0, c], to_feat(ahead))
            send(feat_hbm.at[at], pool.at[4, at], halo_s.at[1, c], halo_r.at[4, c], to_feat(behind))
    send(feat_hbm, pool.at[passed], halo_s.at[2, 0], halo_r.at[passed, 0], to_feat(partner))

    dsum[...] = jnp.zeros_like(dsum)
    loads[0].wait()

    def build(piece, carry):
        owner = lax.rem(me + piece - SPAN + n_feat, n_feat)
        for b in range(num_blocks):
            dst_rows = slice(b * block_len, (b + 1) * block_len)
            for h in range(num_blocks):
                source = owner * num_blocks + h
                acc = jnp.zeros((block_len, block_len), jnp.float32)
                for k in range(num_slots):
                    hit = jnp.logical_and(src_ref[b, k] == source, cnt_ref[b] > k)
                    acc = acc + adj_ref[b, k].astype(jnp.float32) * jnp.where(hit, 1.0, 0.0)
                dsum[dst_rows, :] += acc
                dense[piece, dst_rows, h * block_len : (h + 1) * block_len] = acc.astype(jnp.bfloat16)
        return carry

    def relay():
        for c, at in enumerate(chunks):
            landed(pool.at[x_slot, at], halo_r.at[x_slot, c])
            if square:
                send(pool.at[x_slot, at], pool.at[y_slot, at], halo_s.at[1, c], halo_r.at[y_slot, c], to_feat(y_peer))

    lax.fori_loop(0, SPLIT, build, 0)
    relay()
    lax.fori_loop(SPLIT, WIN, build, 0)
    inv[...] = jnp.broadcast_to(lax.rsqrt(jnp.sum(dsum[...], axis=1, keepdims=True)), inv.shape)
    loads[1].wait()
    loads[2].wait()
    preact[...] = dot_nn(both[0], ws_ref[...])
    summed[...] = dot_nn(dense[SPAN], both[0])
    landed(pool.at[near], halo_r.at[near, 0])
    summed[...] += dot_nn(dense[near], pool[near])
    summed[...] += dot_nn(dense[x_slot], pool[x_slot])
    for c, at in enumerate(chunks):
        landed(pool.at[y_slot, at], halo_r.at[y_slot, c])
        send(pool.at[far, at], pool.at[near, at], halo_s.at[3, c], halo_r.at[near, SPARE + c], to_feat(partner))
    summed[...] += dot_nn(dense[y_slot], pool[y_slot])
    for load in loads[3:]:
        load.wait()
    for c, at in enumerate(chunks):
        landed(pool.at[passed, at], halo_r.at[passed, SPARE + c])
    summed[...] += dot_nn(dense[passed], pool[passed])

    def aggregate(at):
        both[1, at, :] = (summed[at, :] * inv[at, :1]).astype(jnp.bfloat16)

    strips(rows, aggregate)
    preact[...] += dot_nn(both[1], wn_ref[...])
    mult_ref[...] = mult_ref[...] * jnp.exp2(-shift_ref[...].astype(jnp.float32))

    def activate(at):
        scale = mult_ref[...]
        scaled = preact[at, :] * scale
        gate = 1.0 / (1.0 + jnp.exp(-scaled))
        out_ref[at, :] = (scaled * gate).astype(jnp.bfloat16)
        gpre[at, :] = (
            cot_ref[at, :].astype(jnp.float32) * gate * (1.0 + scaled * (1.0 - gate)) * scale
        ).astype(jnp.bfloat16)

    strips(rows, activate)
    stores = []

    def store(src, dst):
        copy = pltpu.make_async_copy(src, dst, store_s.at[len(stores)])
        copy.start()
        stores.append(copy)

    store(out_ref, out_hbm)

    half = buf1.shape[0]
    c2 = buf2.shape[0]
    c3 = c2 // n_grp
    panels = gpre.shape[1] // lanes
    given = dot_tn(both[1 - core], gpre[...])
    for j in range(panels):
        part_out[j * width : (j + 1) * width, :] = given[:, j * lanes : (j + 1) * lanes].astype(jnp.bfloat16)
    order = [lax.rem(chip + j, n_chip) for j in range(1, n_chip + 1)]
    spans = [pl.ds(pl.multiple_of(p * c2, c2), c2) for p in order]
    for j, at in enumerate(spans):
        send(part_out.at[at], part_in.at[at], rs1_s.at[j], rs1_r.at[order[j]], to_feat(partner))
    kept = dot_tn(both[core], gpre[...])
    for j in range(panels):
        part_own[j * width : (j + 1) * width, :] = kept[:, j * lanes : (j + 1) * lanes]

    pulled = dot_nt(gpre[...], wn_ref[...])
    back[...] = (pulled * inv[:, :1]).astype(jnp.bfloat16)
    term_out[passed] = dot_tn(dense[passed], back[...]).astype(jnp.bfloat16)
    send(term_out.at[passed], term_in.at[2], term_s.at[0, 0], term_r.at[2, 0], to_feat(partner))

    for j, at in enumerate(spans):
        landed(part_in.at[at], rs1_r.at[order[j]])
        buf1[at, :] = (part_own[at, :] + part_in[at, :].astype(jnp.float32)).astype(jnp.bfloat16)
    if fine:
        owners = [lax.rem(grp + 1 + q, n_grp) for q in range(n_grp)]
        cuts = [(pl.multiple_of(o * c3, c3), c3) for o in owners]
    else:
        cuts = [(0, c2)]
    for q, (first, size) in enumerate(cuts):
        for j, peer in enumerate(chip_peers):
            src = buf1.at[pl.ds(pl.multiple_of((peer // 2) * c2 + first, 16), size)]
            send(src, in2.at[j, pl.ds(first, size)], rs2_s.at[j, q], rs2_r.at[j, q], to_feat(peer))

    term_sum[0] = dot_tn(dense[x_slot], back[...])
    term_sum[1] = dot_tn(dense[y_slot], back[...])
    landed(term_in.at[2], term_r.at[2, 0])
    through = lax.rem(core + chip, 2)
    term_sum[through] += term_in[2].astype(jnp.float32)
    tstep = rows // 2
    halves = [pl.ds(c * tstep, tstep) for c in range(2)]
    for c, at in enumerate(halves):
        term_out[y_slot, at, :] = term_sum[1, at, :].astype(jnp.bfloat16)
        if square:
            send(term_out.at[y_slot, at], term_in.at[1, at], term_s.at[1, c], term_r.at[1, c], to_feat(y_peer))
        else:
            target = lax.rem(me + y_slot - 2 + n_feat, n_feat)
            send(term_out.at[y_slot, at], term_in.at[odd, at], term_s.at[1, c], term_r.at[odd, c], to_feat(target))
    term_out[near] = dot_tn(dense[near], back[...]).astype(jnp.bfloat16)
    send(term_out.at[near], term_in.at[3], term_s.at[3, 0], term_r.at[3, 0], to_feat(partner))
    own_grad[...] = dot_nt(gpre[...], ws_ref[...])
    own_grad[...] += dot_tn(dense[SPAN], back[...])

    def send_terms():
        for c, at in enumerate(halves):
            value = term_sum[0, at, :]
            if square:
                landed(term_in.at[1, at], term_r.at[1, c])
                value = value + term_in[1, at, :].astype(jnp.float32)
            term_out[x_slot, at, :] = value.astype(jnp.bfloat16)
            if square:
                send(term_out.at[x_slot, at], term_in.at[0, at], term_s.at[2, c], term_r.at[0, c], to_feat(x_peer))
            else:
                target = lax.rem(me + x_slot - 2 + n_feat, n_feat)
                place = 1 - odd
                send(term_out.at[x_slot, at], term_in.at[place, at], term_s.at[2, c], term_r.at[place, c], to_feat(target))

    if not fine:
        send_terms()

    for q, (first, size) in enumerate(cuts):
        at = pl.ds(first, size)
        total = buf1[pl.ds(pl.multiple_of(chip * c2 + first, 16), size), :].astype(jnp.float32)
        for j in range(n_chip - 1):
            landed(in2.at[j, at], rs2_r.at[j, q])
            total = total + in2[j, at, :].astype(jnp.float32)
        buf2[at, :] = total.astype(jnp.bfloat16)
        if fine and q < n_grp - 1:
            send(buf2.at[at], in3.at[q], rs3_s.at[q], rs3_r.at[q], to_grp(grp_peers[q]))
    if fine:
        send_terms()
    else:
        for j, peer in enumerate(grp_peers):
            at = pl.ds(pl.multiple_of(peer * c3, c3), c3)
            send(buf2.at[at], in3.at[j], rs3_s.at[j], rs3_r.at[j], to_grp(peer))
    total = buf2[pl.ds(pl.multiple_of(grp * c3, c3), c3), :].astype(jnp.float32)
    for j in range(n_grp - 1):
        landed(in3.at[j], rs3_r.at[j])
        total = total + in3[j].astype(jnp.float32)

    def piece3(owner):
        return full.at[pl.ds(pl.multiple_of(core * half + chip * c2 + owner * c3, c3), c3)]

    def piece2(side, owner):
        return full.at[pl.ds(pl.multiple_of(side * half + owner * c2, c2), c2)]

    def spread_piece(owner, q):
        for j, peer in enumerate(chip_peers):
            send(piece3(owner), piece3(owner), ag2_s.at[j, q], ag2_r.at[j, q], to_feat(peer))

    piece3(grp)[...] = total.astype(jnp.bfloat16)
    for j, peer in enumerate(grp_peers):
        send(piece3(grp), piece3(grp), ag3_s.at[j], ag3_r.at[j], to_grp(peer))
    if fine:
        spread_piece(grp, 0)
    for j in range(n_grp - 1):
        owner = lax.rem(grp + n_grp - 1 - j, n_grp)
        landed(piece3(owner), ag3_r.at[j])
        if fine:
            spread_piece(owner, j + 1)
    if not fine:
        for j, peer in enumerate(chip_peers):
            send(piece2(core, chip), piece2(core, chip), ag2_s.at[j, 0], ag2_r.at[j, 0], to_feat(peer))
    send(piece2(core, chip), piece2(core, chip), ag1_s.at[0], ag1_r.at[0], to_feat(partner))

    arrivals = (0, 3) if square else (0, 1, 3)
    for slot in arrivals:
        if slot == 3:
            landed(term_in.at[3], term_r.at[3, 0])
        else:
            for c, at in enumerate(halves):
                landed(term_in.at[slot, at], term_r.at[slot, c])

    def finish(at):
        grad = own_grad[at, :]
        for slot in arrivals:
            grad = grad + term_in[slot, at, :].astype(jnp.float32)
        gfeat_ref[at, :] = grad.astype(jnp.bfloat16)

    strips(rows, finish)
    store(gfeat_ref, gfeat_hbm)

    for j in range(n_chip - 1):
        owner = lax.rem(chip + n_chip - 1 - j, n_chip)
        for q in range(len(cuts)):
            if fine:
                piece = full.at[
                    pl.ds(pl.multiple_of(core * half + owner * c2 + lax.rem(grp + n_grp - q, n_grp) * c3, c3), c3)
                ]
            else:
                piece = piece2(core, owner)
            landed(piece, ag2_r.at[j, q])
        send(piece2(core, owner), piece2(core, owner), ag1_s.at[j + 1], ag1_r.at[j + 1], to_feat(partner))
    own_half = pl.ds(pl.multiple_of(core * half, half), half)
    store(full.at[own_half], grads_hbm.at[own_half])
    for j in range(n_chip):
        owner = lax.rem(chip + n_chip - j, n_chip)
        landed(piece2(1 - core, owner), ag1_r.at[j])
    its_half = pl.ds(pl.multiple_of((1 - core) * half, half), half)
    store(full.at[its_half], grads_hbm.at[its_half])
    for copy in sent:
        copy.wait_send()
    for copy in stores:
        copy.wait()


def local(
    n_feat, n_grp, features, adj_tiles, src_block, counts, w_self, w_neigh, multiplier, bit_shift, cotangent
):
    rows, width = features.shape
    hidden = w_self.shape[1]
    n_chip = n_feat // 2
    lanes = hidden if width % (16 * n_chip * n_grp) == 0 else 128
    fine = n_chip * n_grp <= 16
    half = width * hidden // lanes
    c2 = half // n_chip
    c3 = c2 // n_grp
    bf, f32 = jnp.bfloat16, jnp.float32
    smem = pl.BlockSpec(memory_space=pltpu.SMEM)
    hbm = pl.BlockSpec(memory_space=pltpu.HBM)
    dma = pltpu.SemaphoreType.DMA
    cuts = n_grp if fine else 1
    output, grad_features, grads = pl.pallas_call(
        functools.partial(kernel, n_feat, n_grp, fine),
        out_shape=(
            jax.ShapeDtypeStruct((rows, hidden), bf),
            jax.ShapeDtypeStruct((rows, width), bf),
            jax.ShapeDtypeStruct((2 * half, lanes), bf),
        ),
        in_specs=[smem, smem] + [hbm] * 7,
        out_specs=(hbm, hbm, hbm),
        scratch_shapes=[
            pltpu.VMEM((rows, hidden), bf),
            pltpu.VMEM((rows, width), bf),
            pltpu.VMEM(adj_tiles.shape, bf),
            pltpu.VMEM(w_self.shape, bf),
            pltpu.VMEM(w_neigh.shape, bf),
            pltpu.VMEM((1, hidden), f32),
            pltpu.VMEM((1, hidden), jnp.int32),
            pltpu.VMEM((rows, hidden), bf),
            pltpu.VMEM((WIN, rows, width), bf),
            pltpu.VMEM((WIN, rows, rows), bf),
            pltpu.VMEM((rows, adj_tiles.shape[3]), f32),
            pltpu.VMEM((rows, 128), f32),
            pltpu.VMEM((rows, width), f32),
            pltpu.VMEM((rows, hidden), f32),
            pltpu.VMEM((2, rows, width), bf),
            pltpu.VMEM((rows, hidden), bf),
            pltpu.VMEM((half, lanes), bf),
            pltpu.VMEM((half, lanes), f32),
            pltpu.VMEM((half, lanes), bf),
            pltpu.VMEM((half, lanes), bf),
            pltpu.VMEM((n_chip - 1, c2, lanes), bf),
            pltpu.VMEM((c2, lanes), bf),
            pltpu.VMEM((n_grp - 1, c3, lanes), bf),
            pltpu.VMEM((2 * half, lanes), bf),
            pltpu.VMEM((rows, width), bf),
            pltpu.VMEM((WIN, rows, width), bf),
            pltpu.VMEM((2, rows, width), f32),
            pltpu.VMEM((rows, width), f32),
            pltpu.VMEM((4, rows, width), bf),
            dma((7,)), dma((4,)), dma((4, CHUNKS)), dma((WIN, SPARE + CHUNKS)), dma((4, 2)), dma((4, 2)),
            dma((n_chip,)), dma((n_chip,)), dma((n_chip - 1, cuts)), dma((n_chip - 1, cuts)),
            dma((n_grp - 1,)), dma((n_grp - 1,)),
            dma((n_chip,)), dma((n_chip,)), dma((n_chip - 1, cuts)), dma((n_chip - 1, cuts)),
            dma((n_grp - 1,)), dma((n_grp - 1,)),
        ],
        compiler_params=pltpu.CompilerParams(
            collective_id=0, has_side_effects=True, vmem_limit_bytes=62 * 1024 * 1024
        ),
    )(
        src_block, counts, features, adj_tiles, w_self, w_neigh,
        multiplier.reshape(1, hidden), bit_shift.reshape(1, hidden), cotangent,
    )
    grad_scale = 1.0 / math.sqrt(rows * n_grp * n_feat)
    if lanes != hidden:
        grads = grads.reshape(2, hidden // lanes, width, lanes).transpose(0, 2, 1, 3).reshape(2 * width, hidden)
    return (
        output,
        grad_features,
        grads[:width].astype(f32) * grad_scale,
        grads[width:].astype(f32) * grad_scale,
    )


def solution(mesh):
    return jax.shard_map(
        functools.partial(local, mesh.shape["feat"], mesh.shape["grp"]),
        mesh=mesh,
        in_specs=(
            P(("grp", "feat"), None),
            P(("grp", "feat"), None, None, None),
            P(("grp", "feat"), None),
            P(("grp", "feat")),
            P(),
            P(),
            P(),
            P(),
            P(("grp", "feat"), None),
        ),
        out_specs=(P(("grp", "feat"), None), P(("grp", "feat"), None), P(), P()),
        check_vma=False,
    )
```

time: 61.8 us -> 53.5 us (0.87)
  local copies, waits for them, and re-layouts: 10.1 us -> 1.75 us
  other arithmetic: 0.88 us -> 2.85 us
  Pallas kernels: 49.8 us -> 48.1 us
    unnamed x16 -> x6, local copies, waits for them, and re-layouts: 7.29 us -> 1.75 us
    mul x3 -> x0, local copies, waits for them, and re-layouts: 2.84 us -> none  [the longest x2 2.16 us: local(): grads[1].astype(f32) * grad_scale]
    mul x2 -> x1, other arithmetic: 0.88 us -> 2.85 us  [local(): grads[width:].astype(f32) * grad_scale]
    pallas_call x1, Pallas kernels: 49.8 us -> 48.1 us  [local(): pl.pallas_call(functools.partial(kernel, n_feat, n_grp, fine), out_shape=...]
where the time goes in v2:
time: 53.5 us; the launch traced here: 53.3 us
  Pallas kernels  48.1 us (90%)
  other arithmetic  2.85 us (5%)
  local copies, waits for them, and re-layouts  1.75 us (3%)
  between operations  0.65 us (1%)
    pallas_call x1, Pallas kernels, local(): pl.pallas_call(functools.partial(kernel, n_feat, n_grp, fine), out_shape=...  48.1 us
    mul x1, other arithmetic, local(): grads[width:].astype(f32) * grad_scale  2.85 us
    unnamed x6, local copies, waits for them, and re-layouts  1.75 us

profile of v2, /device:TPU:1, one launch (start us, length us, event | category | flops | bytes accessed | tf_op | source)
XLA Modules:
  0.0 53.3 jit_solution(8806498426919624733)
XLA Ops:
  0.6 48.1 %shard_map.120 = (bf16[256,512]{1,0:T(8,128)(2,1)}, bf16[256,512]{1,0:T(8,128)(2,1)}, bf16[1024,512]{1,0:T(8,128)(2,1)}) custom-call(s32[2,16]{1,0:T(2,128)} %src_ref.1, s32[2]{0:T(128)} %cnt_ref.1, bf16[256,512]{1,0:T(8,128)(2,1)} %feat_hbm.1, bf16[2,16,128,128]{3,2,1,0:T(8,128)(2,1)} %adj_hbm.1, bf16[512,512]{1,0:T(8,128)(2,1)} %ws_hbm.1, ...), custom_call_target="tpu_custom_call" | custom-call | tf_op jit(solution)/shard_map/pallas_call | solution.py:367
  48.7 0.0 copy-start.1
  48.7 2.9 %convert_multiply_fusion = (f32[512,512]{1,0:T(8,128)}, f32[512,512]{1,0:T(8,128)}) fusion(bf16[1024,512]{1,0:T(8,128)(2,1)} %get-tuple-element.9), kind=kLoop, calls=%fused_computation | loop fusion | flops 1048576 | bytes 3145728 | tf_op jit(solution)/shard_map/mul | solution.py:426
  51.6 0.0 copy-done.1
  51.6 0.0 copy-start
  51.6 0.7 %copy.15 = bf16[256,512]{1,0:T(8,128)(2,1)} copy(bf16[256,512]{1,0:T(8,128)(2,1)S(1)} %copy-done.1) | data formatting | bytes 524288
  52.3 0.3 copy-done
  52.6 0.7 %copy.16 = bf16[256,512]{1,0:T(8,128)(2,1)} copy(bf16[256,512]{1,0:T(8,128)(2,1)S(1)} %copy-done) | data formatting | bytes 524288
Async XLA Ops:
  48.7 2.9 %copy-start.1 = (bf16[256,512]{1,0:T(8,128)(2,1)S(1)}, bf16[256,512]{1,0:T(8,128)(2,1)}, u32[]{:S(2)}) copy-start(bf16[256,512]{1,0:T(8,128)(2,1)} %get-tuple-element.16) | copy-start | bytes 786436
  51.6 1.0 %copy-start = (bf16[256,512]{1,0:T(8,128)(2,1)S(1)}, bf16[256,512]{1,0:T(8,128)(2,1)}, u32[]{:S(2)}) copy-start(bf16[256,512]{1,0:T(8,128)(2,1)} %get-tuple-element.17) | copy-start | bytes 786436
